TPU v7x, 512 devices: a whole 4x8x8 slice. The times are simulated.
512 devices in a mesh: vocab: 16 (over y, core), docs: 32 (over x, z).
Axes of the slice: x: 4, y: 8, z: 8, core: 2. Of those that a mesh axis runs over, the one named last changes fastest.
Arguments:
- counts: bfloat16 [65536, 4, 128], P(('vocab', 'docs')), may hold values from 0 to 2
- doc_owner: int32 [65536, 4], P(('vocab', 'docs')), may hold values from 0 to 511, all different within a row; in each aligned block of 128 rows (0 to 127, 128 to 255, ...) at most 2 rows name the same one
- doc_sub: int32 [65536, 4], P(('vocab', 'docs')), may hold values from 0 to 7
- doc_len: int32 [65536], P(('vocab', 'docs')), may hold values from 256 to 1023
- first_weight: bfloat16 [524288, 2048], P(('vocab', 'docs')), may hold values from -0.25 to 0.25
- first_bias: float32 [2048], replicated, may hold values from -3 to 3
- head_weight: bfloat16 [2048, 1536], P('vocab', 'docs'), may hold values from -0.125 to 0.125
- head_bias: float32 [1536], replicated, may hold values from -4 to 4
- factor: bfloat16 [1536, 1536], P('vocab', 'docs'), as said below
- noise_draw: bfloat16 [65536, 1536], P(('vocab', 'docs')), may hold values from -5 to 5
Outputs:
- sample: bfloat16 [65536, 1536], P(('vocab', 'docs'))
Inputs may be any that keep to these rules, and one draw needn't show every extreme that they name: `doc_owner`: each document names 4 different owners. The documents of one device name one owner in at most 2 slots, and on some device some owner is named in exactly 2 slots. `factor`: lower triangular; diagonal entries lie between 0.5 and 1.5.
All inputs are finite; a program needn't handle non-finite values.
Results may differ from a plain program's by a relative error of at most 0.0038.
Values may be sent and summed in bfloat16 or wider, within the bound.
No kernel may reach another device: no remote copies, remote signals or barrier semaphores. Data moves between devices by JAX's collectives and lax.ppermute only.
A program may use at most 128 MiB of HBM per device.

v0:
```python
import jax
import jax.numpy as jnp
from jax import lax
from jax.sharding import PartitionSpec as P


def local(
    counts,
    doc_owner,
    doc_sub,
    doc_len,
    first_weight,
    first_bias,
    head_weight,
    head_bias,
    factor,
    noise_draw,
):
    vocab_devices = lax.axis_size("vocab")
    docs_devices = lax.axis_size("docs")
    device_count = vocab_devices * docs_devices
    docs_here, slot_count, block_width = counts.shape
    hidden_width = first_weight.shape[1]
    per_owner = first_weight.shape[0] // block_width
    capacity = max(2, 2 * docs_here * slot_count // device_count)
    owner_flat = doc_owner.reshape(-1)
    onehot = (owner_flat[:, None] == jnp.arange(device_count, dtype=jnp.int32)[None, :]).astype(
        jnp.int32
    )
    position = jnp.sum(jnp.cumsum(onehot, axis=0) * onehot, axis=1) - 1
    slot_index = owner_flat * capacity + position
    flat_rows = counts.reshape(-1, block_width)
    send_rows = (
        jnp.zeros((device_count * capacity, block_width), counts.dtype)
        .at[slot_index]
        .set(flat_rows)
    )
    send_sub = (
        jnp.zeros((device_count * capacity,), jnp.bfloat16)
        .at[slot_index]
        .set(doc_sub.reshape(-1).astype(jnp.bfloat16))
    )
    send_rows = send_rows.reshape(vocab_devices, docs_devices, capacity, block_width)
    send_sub = send_sub.reshape(vocab_devices, docs_devices, capacity)
    got_rows, got_sub = (
        lax.all_to_all(
            lax.all_to_all(send_rows, "vocab", split_axis=0, concat_axis=0, tiled=True),
            "docs",
            split_axis=1,
            concat_axis=1,
            tiled=True,
        ),
        lax.all_to_all(
            lax.all_to_all(send_sub, "vocab", split_axis=0, concat_axis=0, tiled=True),
            "docs",
            split_axis=1,
            concat_axis=1,
            tiled=True,
        ),
    )
    got_rows = got_rows.reshape(-1, block_width)
    got_sub = got_sub.reshape(-1).astype(jnp.int32)
    select = (got_sub[:, None] == jnp.arange(per_owner, dtype=jnp.int32)[None, :]).astype(
        jnp.bfloat16
    )
    spread = (select[:, :, None] * got_rows[:, None, :]).reshape(-1, per_owner * block_width)
    owner_terms = jnp.dot(spread, first_weight, preferred_element_type=jnp.float32).astype(
        jnp.bfloat16
    )
    owner_terms = owner_terms.reshape(vocab_devices, docs_devices, capacity, hidden_width)
    returned = lax.all_to_all(
        lax.all_to_all(owner_terms, "vocab", split_axis=0, concat_axis=0, tiled=True),
        "docs",
        split_axis=1,
        concat_axis=1,
        tiled=True,
    )
    returned = returned.reshape(-1, hidden_width)
    own_rows = returned[slot_index].reshape(docs_here, slot_count, hidden_width).astype(jnp.float32)
    summed = jnp.sum(own_rows, axis=1)
    length_scale = 128.0 * slot_count / doc_len.astype(jnp.float32)
    hidden = jax.nn.softplus(summed * length_scale[:, None] + first_bias).astype(jnp.bfloat16)
    panel_rows = lax.all_gather(head_weight, "docs", axis=1, tiled=True)
    location = jnp.dot(
        hidden,
        lax.all_gather(panel_rows, "vocab", axis=0, tiled=True),
        preferred_element_type=jnp.float32,
    )
    factor_panel = lax.all_gather(factor, "docs", axis=1, tiled=True)
    correlated = lax.dot_general(
        noise_draw,
        lax.all_gather(factor_panel, "vocab", axis=0, tiled=True),
        (((1,), (1,)), ((), ())),
        preferred_element_type=jnp.float32,
    )
    return (location + head_bias + correlated).astype(jnp.bfloat16)


def solution(mesh):
    return jax.shard_map(
        local,
        mesh=mesh,
        in_specs=(
            P(("vocab", "docs"), None, None),
            P(("vocab", "docs"), None),
            P(("vocab", "docs"), None),
            P(("vocab", "docs")),
            P(("vocab", "docs"), None),
            P(),
            P("vocab", "docs"),
            P(),
            P("vocab", "docs"),
            P(("vocab", "docs"), None),
        ),
        out_specs=P(("vocab", "docs"), None),
        check_vma=False,
    )
```

profile of v0, /device:TPU:1, one launch (start us, length us, event | category | flops | bytes accessed | tf_op | source)
XLA Modules:
  0.0 425.2 jit_solution(10619048773508162734)
XLA Ops:
  6.5 50.0 %all_gather.12 = bf16[128,1536]{0,1:T(8,128)(2,1)} all-gather(bf16[128,48]{0,1:T(8,128)(2,1)} %param.16), channel_id=1, replica_groups=mesh['vocab'=16,'docs'=32] {'docs'}, dimensions={1}, use_global_device_ids=true | all-gather | bytes 405504 | tf_op jit(solution)/shard_map/all_gather | solution.py:83
  56.6 0.8 copy.58
  57.4 0.1 eq.46
  57.5 0.1 eq.42
  57.6 0.1 copy.60
  57.7 0.3 fusion.5
  58.1 0.1 broadcast_add_fusion
  58.2 0.3 copy.61
  58.5 0.1 copy.57
  58.6 0.1 mul.48
  58.8 0.1 copy.62
  58.9 0.1 reshape.128
  59.0 0.3 fusion.4
  59.3 3.8 scatter_custom_fusion
  63.1 0.3 reshape.109
  63.3 0.8 copy.63
  64.1 18.7 %all-to-all-start = ((bf16[16,32,2]{1,2,0:T(2,128)(2,1)}), bf16[16,32,2]{1,2,0:T(2,128)(2,1)S(1)}, u32[]{:S(2)}, u32[]{:S(2)}) async-start(bf16[16,32,2]{1,2,0:T(2,128)(2,1)} %copy.63), calls=%async_computation | async-start | bytes 16384 | tf_op jit(solution)/shard_map/all_to_all | solution.py:54
  82.9 2.8 scatter_custom_fusion.1
  85.6 4.3 %all-to-all-done = bf16[16,32,2]{1,2,0:T(2,128)(2,1)S(1)} async-done(((bf16[16,32,2]{1,2,0:T(2,128)(2,1)}), bf16[16,32,2]{1,2,0:T(2,128)(2,1)S(1)}, u32[]{:S(2)}, u32[]{:S(2)}) %all-to-all-start) | async-done | bytes 2080 | tf_op jit(solution)/shard_map/all_to_all | solution.py:54
  90.0 3.9 all-to-all-start.2
  93.9 0.7 copy.64
  94.5 13.3 %all-to-all-done.2 = bf16[16,32,2,128]{3,2,1,0:T(2,128)(2,1)S(1)} async-done(((bf16[16,32,2,128]{3,2,1,0:T(2,128)(2,1)}), bf16[16,32,2,128]{3,2,1,0:T(2,128)(2,1)S(1)}, u32[]{:S(2)}, u32[]{:S(2)}) %all-to-all-start.2) | async-done | bytes 262176 | tf_op jit(solution)/shard_map/all_to_all | solution.py:47
  107.9 4.7 %all-to-all-start.1 = ((bf16[16,32,2]{0,2,1:T(2,128)(2,1)}), bf16[16,32,2]{0,2,1:T(2,128)(2,1)S(1)}, u32[]{:S(2)}, u32[]{:S(2)}) async-start(bf16[16,32,2]{0,2,1:T(2,128)(2,1)} %copy.64), calls=%async_computation.1 | async-start | bytes 32768 | tf_op jit(solution)/shard_map/all_to_all | solution.py:53
  112.6 0.9 copy.67
  113.5 7.7 %all-to-all-done.1 = bf16[16,32,2]{0,2,1:T(2,128)(2,1)S(1)} async-done(((bf16[16,32,2]{0,2,1:T(2,128)(2,1)}), bf16[16,32,2]{0,2,1:T(2,128)(2,1)S(1)}, u32[]{:S(2)}, u32[]{:S(2)}) %all-to-all-start.1) | async-done | bytes 2080 | tf_op jit(solution)/shard_map/all_to_all | solution.py:53
  121.2 4.0 all-to-all-start.3
  125.4 0.2 copy.66
  125.6 0.2 reshape.114
  125.7 0.2 fusion.12
  126.0 8.8 %all-to-all-done.3 = bf16[16,32,2,128]{3,2,0,1:T(2,128)(2,1)S(1)} async-done(((bf16[16,32,2,128]{3,2,0,1:T(2,128)(2,1)}), bf16[16,32,2,128]{3,2,0,1:T(2,128)(2,1)S(1)}, u32[]{:S(2)}, u32[]{:S(2)}) %all-to-all-start.3) | async-done | bytes 262176 | tf_op jit(solution)/shard_map/all_to_all | solution.py:46
  134.8 0.2 copy.68
  135.0 3.5 broadcast_multiply_fusion
  138.5 8.3 %convolution_convert_fusion = bf16[1024,2048]{1,0:T(8,128)(2,1)} fusion(bf16[1024,2048]{1,0:T(8,128)(2,1)} %param.14, bf16[128,8,8,128]{3,2,1,0:T(8,128)(2,1)S(1)} %bitcast.26), kind=kOutput, calls=%fused_computation.3 | convolution fusion | flops 4297064448 | bytes 10485760 | tf_op jit(solution)/shard_map/dot_general | solution.py:67
  146.8 7.6 %reshape.112 = bf16[16,32,2,2048]{3,2,1,0:T(2,128)(2,1)} reshape(bf16[1024,2048]{1,0:T(8,128)(2,1)} %convolution_convert_fusion) | data formatting | bytes 8388608 | tf_op jit(solution)/shard_map/reshape | solution.py:70
  154.4 8.1 %all-to-all-start.4 = ((bf16[16,32,2,2048]{3,2,1,0:T(2,128)(2,1)}), bf16[16,32,2,2048]{3,2,1,0:T(2,128)(2,1)}, u32[]{:S(2)}, u32[]{:S(2)}) async-start(bf16[16,32,2,2048]{3,2,1,0:T(2,128)(2,1)} %reshape.112), calls=%async_computation.4 | async-start | bytes 8388608 | tf_op jit(solution)/shard_map/all_to_all | solution.py:72
  162.5 40.7 %all_gather.14 = bf16[96,1536]{0,1:T(8,128)(2,1)S(1)} all-gather(bf16[96,48]{0,1:T(8,128)(2,1)S(1)} %copy-done.1), channel_id=1, replica_groups=mesh['vocab'=16,'docs'=32] {'docs'}, dimensions={1}, use_global_device_ids=true | all-gather | bytes 304128 | tf_op jit(solution)/shard_map/all_gather | solution.py:89
  203.3 0.9 copy.71
  204.2 65.5 %all-to-all-done.4 = bf16[16,32,2,2048]{3,2,1,0:T(2,128)(2,1)} async-done(((bf16[16,32,2,2048]{3,2,1,0:T(2,128)(2,1)}), bf16[16,32,2,2048]{3,2,1,0:T(2,128)(2,1)}, u32[]{:S(2)}, u32[]{:S(2)}) %all-to-all-start.4) | async-done | bytes 4194336 | tf_op jit(solution)/shard_map/all_to_all | solution.py:72
  269.7 8.8 %copy.69 = bf16[16,32,2,2048]{3,2,0,1:T(2,128)(2,1)} copy(bf16[16,32,2,2048]{3,2,1,0:T(2,128)(2,1)} %all-to-all-done.4) | data formatting | bytes 8388608 | tf_op jit(solution)/shard_map/all_to_all | solution.py:72
  278.5 5.2 %all-to-all-start.5 = ((bf16[16,32,2,2048]{3,2,0,1:T(2,128)(2,1)}), bf16[16,32,2,2048]{3,2,0,1:T(2,128)(2,1)}, u32[]{:S(2)}, u32[]{:S(2)}) async-start(bf16[16,32,2,2048]{3,2,0,1:T(2,128)(2,1)} %copy.69), calls=%async_computation.5 | async-start | bytes 8388608 | tf_op jit(solution)/shard_map/all_to_all | solution.py:71
  283.8 94.4 %all-to-all-done.5 = bf16[16,32,2,2048]{3,2,0,1:T(2,128)(2,1)} async-done(((bf16[16,32,2,2048]{3,2,0,1:T(2,128)(2,1)}), bf16[16,32,2,2048]{3,2,0,1:T(2,128)(2,1)}, u32[]{:S(2)}, u32[]{:S(2)}) %all-to-all-start.5) | async-done | bytes 4194336 | tf_op jit(solution)/shard_map/all_to_all | solution.py:71
  378.2 8.0 %copy.70 = bf16[16,32,2,2048]{3,2,1,0:T(2,128)(2,1)} copy(bf16[16,32,2,2048]{3,2,0,1:T(2,128)(2,1)} %all-to-all-done.5) | data formatting | bytes 8388608 | tf_op jit(solution)/shard_map/all_to_all | solution.py:71
  386.2 7.2 %reshape.113 = bf16[1024,2048]{1,0:T(8,128)(2,1)} reshape(bf16[16,32,2,2048]{3,2,1,0:T(2,128)(2,1)} %copy.70) | data formatting | bytes 8388608 | tf_op jit(solution)/shard_map/reshape | solution.py:78
  393.4 7.1 %gather_fusion = bf16[512,2048]{1,0:T(8,128)(2,1)S(1)} fusion(bf16[1024,2048]{1,0:T(8,128)(2,1)} %reshape.113, s32[1024]{0:T(1024)S(1)} %pad_clamp_fusion), kind=kCustom, calls=%fused_computation | custom fusion | bytes 4196352 | tf_op jit(solution)/shard_map/gather | solution.py:79
  400.6 3.0 reshape.115
  403.6 4.8 %reduce_sum.19 = f32[128,2048]{1,0:T(8,128)S(1)} reduce(f32[128,4,2048]{2,1,0:T(4,128)} %reshape.115, f32[]{:T(128)} %constant.6.clone.1), dimensions={1}, to_apply=%region_5.6 | reduce | flops 786432 | bytes 5242884 | tf_op jit(solution)/shard_map/reduce_sum | solution.py:80
  408.5 5.1 %convolution_add_fusion.1 = f32[128,1536]{1,0:T(8,128)S(1)} fusion(bf16[2048,1536]{0,1:T(8,128)(2,1)} %all-gather.3.cloned.1.call-done, f32[128,2048]{1,0:T(8,128)S(1)} %reduce_sum.19, f32[2048]{0:T(1024)S(1)} %copy-done.4, f32[128]{0:T(128)S(1)} %convert_divide_fusion, f32[1536]{0:T(1024)S(1)} %copy-done.5), kind=kOutput, calls=%fused_computation.6 | convolution fusion | flops 807862272 | bytes 8141312 | tf_op jit(solution)/shard_map/dot_general | solution.py:84
  413.7 4.7 %fusion = bf16[128,1536]{1,0:T(8,128)(2,1)} fusion(f32[128,1536]{1,0:T(8,128)S(1)} %convolution_add_fusion.1, bf16[128,1536]{1,0:T(8,128)(2,1)S(1)} %copy-done, bf16[1536,1536]{1,0:T(8,128)(2,1)} %all-gather.5.cloned.1.call-done), kind=kOutput, calls=%fused_computation.7 | convolution fusion | flops 604372992 | bytes 6291456 | tf_op jit(solution)/shard_map/dot_general | solution.py:90
  (32 shorter events, 0.3 us)
Async XLA Ops:
  6.5 407.1 %copy-start = (bf16[128,1536]{1,0:T(8,128)(2,1)S(1)}, bf16[128,1536]{1,0:T(8,128)(2,1)}, u32[]{:S(2)}) copy-start(bf16[128,1536]{1,0:T(8,128)(2,1)} %param.19) | copy-start | bytes 1179652
  6.5 52.0 %copy-start.2 = (s32[128,4]{0,1:T(4,128)S(1)}, s32[128,4]{0,1:T(4,128)}, u32[]{:S(2)}) copy-start(s32[128,4]{0,1:T(4,128)} %param.11) | copy-start | bytes 6148
  6.5 52.2 %copy-start.3 = (s32[128,4]{0,1:T(4,128)S(1)}, s32[128,4]{0,1:T(4,128)}, u32[]{:S(2)}) copy-start(s32[128,4]{0,1:T(4,128)} %param.12) | copy-start | bytes 6148
  6.5 402.0 %all-gather.3.cloned.1.call-start = ((), (), s32[]{:S(2)}) async-start(), calls=%async_computation.6 | async-start | bytes 6684672 | tf_op jit(solution)/shard_map/all_gather | solution.py:86
  64.1 25.8 %all-to-all-start = ((bf16[16,32,2]{1,2,0:T(2,128)(2,1)}), bf16[16,32,2]{1,2,0:T(2,128)(2,1)S(1)}, u32[]{:S(2)}, u32[]{:S(2)}) async-start(bf16[16,32,2]{1,2,0:T(2,128)(2,1)} %copy.63), calls=%async_computation | async-start | bytes 16384 | tf_op jit(solution)/shard_map/all_to_all | solution.py:54
  90.0 17.9 %all-to-all-start.2 = ((bf16[16,32,2,128]{3,2,1,0:T(2,128)(2,1)}), bf16[16,32,2,128]{3,2,1,0:T(2,128)(2,1)S(1)}, u32[]{:S(2)}, u32[]{:S(2)}) async-start(bf16[16,32,2,128]{3,2,1,0:T(2,128)(2,1)} %bitcast.6), calls=%async_computation.2 | async-start | bytes 524288 | tf_op jit(solution)/shard_map/all_to_all | solution.py:47
  107.9 13.3 %all-to-all-start.1 = ((bf16[16,32,2]{0,2,1:T(2,128)(2,1)}), bf16[16,32,2]{0,2,1:T(2,128)(2,1)S(1)}, u32[]{:S(2)}, u32[]{:S(2)}) async-start(bf16[16,32,2]{0,2,1:T(2,128)(2,1)} %copy.64), calls=%async_computation.1 | async-start | bytes 32768 | tf_op jit(solution)/shard_map/all_to_all | solution.py:53
  121.2 13.5 %all-to-all-start.3 = ((bf16[16,32,2,128]{3,2,0,1:T(2,128)(2,1)}), bf16[16,32,2,128]{3,2,0,1:T(2,128)(2,1)S(1)}, u32[]{:S(2)}, u32[]{:S(2)}) async-start(bf16[16,32,2,128]{3,2,0,1:T(2,128)(2,1)} %copy.67), calls=%async_computation.3 | async-start | bytes 524288 | tf_op jit(solution)/shard_map/all_to_all | solution.py:46
  154.4 8.1 %copy-start.1 = (bf16[96,48]{0,1:T(8,128)(2,1)S(1)}, bf16[96,48]{0,1:T(8,128)(2,1)}, u32[]{:S(2)}) copy-start(bf16[96,48]{0,1:T(8,128)(2,1)} %param.18) | copy-start | bytes 27652
  154.4 115.3 %all-to-all-start.4 = ((bf16[16,32,2,2048]{3,2,1,0:T(2,128)(2,1)}), bf16[16,32,2,2048]{3,2,1,0:T(2,128)(2,1)}, u32[]{:S(2)}, u32[]{:S(2)}) async-start(bf16[16,32,2,2048]{3,2,1,0:T(2,128)(2,1)} %reshape.112), calls=%async_computation.4 | async-start | bytes 8388608 | tf_op jit(solution)/shard_map/all_to_all | solution.py:72
  162.5 251.2 %all-gather.5.cloned.1.call-start = ((), (), s32[]{:S(2)}) async-start(), calls=%async_computation.7 | async-start | bytes 5013504 | tf_op jit(solution)/shard_map/all_gather | solution.py:92
  278.5 5.2 %copy-start.6 = (s32[128]{0:T(128)S(1)}, s32[128]{0:T(128)}, u32[]{:S(2)}) copy-start(s32[128]{0:T(128)} %param.13) | copy-start | bytes 1540
  278.5 99.7 %all-to-all-start.5 = ((bf16[16,32,2,2048]{3,2,0,1:T(2,128)(2,1)}), bf16[16,32,2,2048]{3,2,0,1:T(2,128)(2,1)}, u32[]{:S(2)}, u32[]{:S(2)}) async-start(bf16[16,32,2,2048]{3,2,0,1:T(2,128)(2,1)} %copy.69), calls=%async_computation.5 | async-start | bytes 8388608 | tf_op jit(solution)/shard_map/all_to_all | solution.py:71
  403.6 4.9 %copy-start.4 = (f32[2048]{0:T(1024)S(1)}, f32[2048]{0:T(1024)}, u32[]{:S(2)}) copy-start(f32[2048]{0:T(1024)} %param.15) | copy-start | bytes 24580
  403.6 4.9 %copy-start.5 = (f32[1536]{0:T(1024)S(1)}, f32[1536]{0:T(1024)}, u32[]{:S(2)}) copy-start(f32[1536]{0:T(1024)} %param.17) | copy-start | bytes 18436
Sparse Core Ops, SparseCore 0:
  56.7 72.7 all-gather.2
  204.3 78.6 all-gather.4
where the time goes:
time: 426 us; the launch traced here: 425 us
  waiting for transfers between devices  194 us (46%)
  blocking collectives  90.8 us (21%)
  local copies, waits for them, and re-layouts  54.5 us (13%)
  starting transfers between devices  44.7 us (10%)
  matrix products  18.1 us (4%)
  between operations  13.7 us (3%)
  other arithmetic  9.24 us (2%)
    all_to_all x1, waiting for transfers between devices, local(): lax.all_to_all(lax.all_to_all(owner_terms, 'vocab', split_axis=0, concat_...  94.4 us
    all_to_all x1, waiting for transfers between devices, local(): lax.all_to_all(owner_terms, 'vocab', split_axis=0, concat_axis=0, tiled=T...  65.5 us
    all_gather x1, blocking collectives, local(): panel_rows = lax.all_gather(head_weight, 'docs', axis=1, tiled=True)  50 us
    all_gather x1, blocking collectives, local(): factor_panel = lax.all_gather(factor, 'docs', axis=1, tiled=True)  40.7 us
    all_to_all x1, starting transfers between devices, local(): lax.all_to_all(send_sub, 'vocab', split_axis=0, concat_axis=0, tiled=True)  18.7 us
    all_to_all x1, waiting for transfers between devices, local(): lax.all_to_all(send_rows, 'vocab', split_axis=0, concat_axis=0, tiled=True)  13.3 us
    all_to_all x1, waiting for transfers between devices, local(): lax.all_to_all(lax.all_to_all(send_rows, 'vocab', split_axis=0, concat_ax...  8.81 us
    all_to_all x1, local copies, waits for them, and re-layouts, local(): lax.all_to_all(owner_terms, 'vocab', split_axis=0, concat_axis=0, tiled=T...  8.8 us
  transfers between devices with their start and end apart: 8, of which 6 were waited for; matrix products, arithmetic and copies ran while one was open for 18% of the time, Pallas kernels for 0%

commit v1 on v0

--- a/solution.py
+++ b/solution.py
@@ -2,6 +2,19 @@
 import jax.numpy as jnp
 from jax import lax
 from jax.sharding import PartitionSpec as P
+
+
+def gather_around(array, axis, dim):
+    ways = lax.axis_size(axis)
+    up = [(d, (d + 1) % ways) for d in range(ways)]
+    down = [(d, (d - 1) % ways) for d in range(ways)]
+    earlier, later = ([array], [array])
+    for _ in range(ways // 2):
+        earlier.append(lax.ppermute(earlier[-1], axis, up))
+    for _ in range((ways - 1) // 2):
+        later.append(lax.ppermute(later[-1], axis, down))
+    line = jnp.concatenate([*earlier[::-1], *later[1:]], axis=dim)
+    return jnp.roll(line, (lax.axis_index(axis) - ways // 2) * array.shape[dim], axis=dim)
 
 
 def local(
@@ -82,9 +95,7 @@
     hidden = jax.nn.softplus(summed * length_scale[:, None] + first_bias).astype(jnp.bfloat16)
     panel_rows = lax.all_gather(head_weight, "docs", axis=1, tiled=True)
     location = jnp.dot(
-        hidden,
-        lax.all_gather(panel_rows, "vocab", axis=0, tiled=True),
-        preferred_element_type=jnp.float32,
+        hidden, gather_around(panel_rows, "vocab", 0), preferred_element_type=jnp.float32
     )
     factor_panel = lax.all_gather(factor, "docs", axis=1, tiled=True)
     correlated = lax.dot_general(

time: 426 us -> 466 us (1.094); the launches traced: 425 us -> 457 us
  waiting for transfers between devices: 194 us -> 132 us
  starting transfers between devices: 44.7 us -> 106 us
  local copies, waits for them, and re-layouts: 54.5 us -> 94.7 us
  blocking collectives: 90.8 us -> 81.4 us
    all_to_all x1, waiting for transfers between devices: 65.5 us -> 0.01 us  [local(): lax.all_to_all(owner_terms, 'vocab', split_axis=0, concat_axis=0, tiled=T...]
    ppermute x0 -> x15, starting transfers between devices: none -> 63 us  [the longest x7 40.9 us: gather_around(): later.append(lax.ppermute(later[-1], axis, down))]
    ppermute x0 -> x15, waiting for transfers between devices: none -> 56.8 us  [the longest x8 52.6 us: gather_around(): earlier.append(lax.ppermute(earlier[-1], axis, up))]
    all_to_all x1, waiting for transfers between devices: 94.4 us -> 43.1 us  [local(): lax.all_to_all(lax.all_to_all(owner_terms, 'vocab', split_axis=0, concat_...]
    unnamed x16 -> x51, local copies, waits for them, and re-layouts: 0.82 us -> 39.3 us
    all_gather x1, blocking collectives: 50 us -> 40.7 us  [local(): panel_rows = lax.all_gather(head_weight, 'docs', axis=1, tiled=True)]
    all_to_all x1, starting transfers between devices: 18.7 us -> 10.1 us  [local(): lax.all_to_all(send_sub, 'vocab', split_axis=0, concat_axis=0, tiled=True)]
    all_to_all x1, starting transfers between devices: 4.7 us -> 11.3 us  [local(): lax.all_to_all(lax.all_to_all(send_sub, 'vocab', split_axis=0, concat_axi...]
  transfers between devices with their start and end apart: 8 -> 22, of which waited for: 6 -> 13; matrix products, arithmetic and copies ran while one was open for 18% -> 13% of each run, Pallas kernels for 0% -> 0%
where the time goes in v1:
time: 466 us; the launch traced here: 457 us
  waiting for transfers between devices  132 us (28%)
  starting transfers between devices  106 us (23%)
  local copies, waits for them, and re-layouts  94.7 us (20%)
  blocking collectives  81.4 us (17%)
  matrix products  18.1 us (4%)
  between operations  13.6 us (3%)
  other arithmetic  11.3 us (2%)
    ppermute x8, waiting for transfers between devices, gather_around(): earlier.append(lax.ppermute(earlier[-1], axis, up))  52.6 us
    all_to_all x1, waiting for transfers between devices, local(): lax.all_to_all(lax.all_to_all(owner_terms, 'vocab', split_axis=0, concat_...  43.1 us
    ppermute x7, starting transfers between devices, gather_around(): later.append(lax.ppermute(later[-1], axis, down))  40.9 us
    all_gather x1, blocking collectives, local(): factor_panel = lax.all_gather(factor, 'docs', axis=1, tiled=True)  40.7 us
    all_gather x1, blocking collectives, local(): panel_rows = lax.all_gather(head_weight, 'docs', axis=1, tiled=True)  40.7 us
    unnamed x51, local copies, waits for them, and re-layouts  39.3 us
    ppermute x8, starting transfers between devices, gather_around(): earlier.append(lax.ppermute(earlier[-1], axis, up))  22.1 us
    all_to_all x1, starting transfers between devices, local(): lax.all_to_all(lax.all_to_all(send_sub, 'vocab', split_axis=0, concat_axi...  11.3 us
  transfers between devices with their start and end apart: 22, of which 13 were waited for; matrix products, arithmetic and copies ran while one was open for 13% of the time, Pallas kernels for 0%

profile of v1, /device:TPU:1, one launch (start us, length us, event | category | flops | bytes accessed | tf_op | source)
XLA Modules:
  0.0 456.5 jit_solution(10180993587252881399)
XLA Ops:
  10.6 3.8 scatter_custom_fusion
  15.4 10.1 %all-to-all-start = ((bf16[16,32,2]{1,2,0:T(2,128)(2,1)}), bf16[16,32,2]{1,2,0:T(2,128)(2,1)S(1)}, u32[]{:S(2)}, u32[]{:S(2)}) async-start(bf16[16,32,2]{1,2,0:T(2,128)(2,1)} %copy.63), calls=%async_computation | async-start | bytes 16384 | tf_op jit(solution)/shard_map/all_to_all | solution.py:67
  25.6 2.8 scatter_custom_fusion.1
  28.4 4.3 all-to-all-done
  32.7 4.0 all-to-all-start.2
  37.3 11.2 %all-to-all-done.2 = bf16[16,32,2,128]{3,2,1,0:T(2,128)(2,1)S(1)} async-done(((bf16[16,32,2,128]{3,2,1,0:T(2,128)(2,1)}), bf16[16,32,2,128]{3,2,1,0:T(2,128)(2,1)S(1)}, u32[]{:S(2)}, u32[]{:S(2)}) %all-to-all-start.2) | async-done | bytes 262176 | tf_op jit(solution)/shard_map/all_to_all | solution.py:60
  48.5 11.3 %all-to-all-start.1 = ((bf16[16,32,2]{0,2,1:T(2,128)(2,1)}), bf16[16,32,2]{0,2,1:T(2,128)(2,1)S(1)}, u32[]{:S(2)}, u32[]{:S(2)}) async-start(bf16[16,32,2]{0,2,1:T(2,128)(2,1)} %copy.64), calls=%async_computation.1 | async-start | bytes 32768 | tf_op jit(solution)/shard_map/all_to_all | solution.py:66
  60.7 7.7 %all-to-all-done.1 = bf16[16,32,2]{0,2,1:T(2,128)(2,1)S(1)} async-done(((bf16[16,32,2]{0,2,1:T(2,128)(2,1)}), bf16[16,32,2]{0,2,1:T(2,128)(2,1)S(1)}, u32[]{:S(2)}, u32[]{:S(2)}) %all-to-all-start.1) | async-done | bytes 2080 | tf_op jit(solution)/shard_map/all_to_all | solution.py:66
  68.4 4.1 all-to-all-start.3
  73.1 8.8 %all-to-all-done.3 = bf16[16,32,2,128]{3,2,0,1:T(2,128)(2,1)S(1)} async-done(((bf16[16,32,2,128]{3,2,0,1:T(2,128)(2,1)}), bf16[16,32,2,128]{3,2,0,1:T(2,128)(2,1)S(1)}, u32[]{:S(2)}, u32[]{:S(2)}) %all-to-all-start.3) | async-done | bytes 262176 | tf_op jit(solution)/shard_map/all_to_all | solution.py:59
  82.2 3.5 broadcast_multiply_fusion
  85.7 8.3 %convolution_convert_fusion = bf16[1024,2048]{1,0:T(8,128)(2,1)} fusion(bf16[1024,2048]{1,0:T(8,128)(2,1)} %param.14, bf16[128,8,8,128]{3,2,1,0:T(8,128)(2,1)S(1)} %bitcast.25), kind=kOutput, calls=%fused_computation.5 | convolution fusion | flops 4297064448 | bytes 10485760 | tf_op jit(solution)/shard_map/dot_general | solution.py:80
  94.0 7.6 %reshape.112 = bf16[16,32,2,2048]{3,2,1,0:T(2,128)(2,1)} reshape(bf16[1024,2048]{1,0:T(8,128)(2,1)} %convolution_convert_fusion) | data formatting | bytes 8388608 | tf_op jit(solution)/shard_map/reshape | solution.py:83
  101.7 7.9 %all-to-all-start.4 = ((bf16[16,32,2,2048]{3,2,1,0:T(2,128)(2,1)}), bf16[16,32,2,2048]{3,2,1,0:T(2,128)(2,1)}, u32[]{:S(2)}, u32[]{:S(2)}) async-start(bf16[16,32,2,2048]{3,2,1,0:T(2,128)(2,1)} %reshape.112), calls=%async_computation.4 | async-start | bytes 8388608 | tf_op jit(solution)/shard_map/all_to_all | solution.py:85
  109.6 40.7 %all_gather.9 = bf16[128,1536]{0,1:T(8,128)(2,1)S(1)} all-gather(bf16[128,48]{0,1:T(8,128)(2,1)S(1)} %copy-done.5), channel_id=1, replica_groups=mesh['vocab'=16,'docs'=32] {'docs'}, dimensions={1}, use_global_device_ids=true | all-gather | bytes 405504 | tf_op jit(solution)/shard_map/all_gather | solution.py:96
  150.3 8.9 %collective-permute-start = (bf16[128,1536]{0,1:T(8,128)(2,1)S(1)}, bf16[128,1536]{0,1:T(8,128)(2,1)S(1)}, u32[]{:S(2)}, u32[]{:S(2)}) collective-permute-start(bf16[128,1536]{0,1:T(8,128)(2,1)S(1)} %all_gather.9), channel_id=1, source_target_pairs={{0,32},{32,64},{64,96},{96,128},{128,160},{160,192},{192,224},{224... | collective-permute-start | bytes 1179656 | tf_op jit(solution)/shard_map/ppermute | solution.py:13
  159.3 45.4 %collective-permute-done = bf16[128,1536]{0,1:T(8,128)(2,1)S(1)} collective-permute-done((bf16[128,1536]{0,1:T(8,128)(2,1)S(1)}, bf16[128,1536]{0,1:T(8,128)(2,1)S(1)}, u32[]{:S(2)}, u32[]{:S(2)}) %collective-permute-start) | collective-permute-done | bytes 393248 | tf_op jit(solution)/shard_map/ppermute | solution.py:13
  204.6 2.5 collective-permute-start.1
  208.3 3.6 collective-permute-done.1
  211.8 2.5 collective-permute-start.2
  214.6 2.1 collective-permute-start.9
  216.7 2.4 collective-permute-done.2
  219.0 2.5 collective-permute-start.3
  222.1 3.0 collective-permute-start.10
  226.3 2.4 collective-permute-start.4
  228.7 40.7 %all_gather.10 = bf16[96,1536]{0,1:T(8,128)(2,1)} all-gather(bf16[96,48]{0,1:T(8,128)(2,1)S(1)} %copy-done.6), channel_id=1, replica_groups=mesh['vocab'=16,'docs'=32] {'docs'}, dimensions={1}, use_global_device_ids=true | all-gather | bytes 304128 | tf_op jit(solution)/shard_map/all_gather | solution.py:100
  269.5 1.9 copy.71
  271.4 16.1 %collective-permute-start.11 = (bf16[128,1536]{0,1:T(8,128)(2,1)S(1)}, bf16[128,1536]{0,1:T(8,128)(2,1)S(1)}, u32[]{:S(2)}, u32[]{:S(2)}) collective-permute-start(bf16[128,1536]{0,1:T(8,128)(2,1)S(1)} %collective-permute-done.10), channel_id=1, source_target_pairs={{0,480},{32,0},{64,32},{96,64},{128,96},{160,128},{192,160},{224,1... | collective-permute-start | bytes 1179656 | tf_op jit(solution)/shard_map/ppermute | solution.py:15
  289.5 4.0 collective-permute-start.12
  294.9 2.0 collective-permute-done.12
  296.9 10.5 %collective-permute-start.13 = (bf16[128,1536]{0,1:T(8,128)(2,1)}, bf16[128,1536]{0,1:T(8,128)(2,1)}, u32[]{:S(2)}, u32[]{:S(2)}) collective-permute-start(bf16[128,1536]{0,1:T(8,128)(2,1)} %collective-permute-done.12), channel_id=1, source_target_pairs={{0,480},{32,0},{64,32},{96,64},{128,96},{160,128},{192,160},{224,1... | collective-permute-start | bytes 1179656 | tf_op jit(solution)/shard_map/ppermute | solution.py:15
  307.4 1.9 collective-permute-start.7
  309.3 8.8 %copy.69 = bf16[16,32,2,2048]{3,2,0,1:T(2,128)(2,1)} copy(bf16[16,32,2,2048]{3,2,1,0:T(2,128)(2,1)} %all-to-all-done.4) | data formatting | bytes 8388608 | tf_op jit(solution)/shard_map/all_to_all | solution.py:85
  318.1 5.1 %all-to-all-start.5 = ((bf16[16,32,2,2048]{3,2,0,1:T(2,128)(2,1)}), bf16[16,32,2,2048]{3,2,0,1:T(2,128)(2,1)}, u32[]{:S(2)}, u32[]{:S(2)}) async-start(bf16[16,32,2,2048]{3,2,0,1:T(2,128)(2,1)} %copy.69), calls=%async_computation.5 | async-start | bytes 8388608 | tf_op jit(solution)/shard_map/all_to_all | solution.py:84
  323.9 4.2 collective-permute-start.14
  329.9 1.8 constant_dynamic-update-slice_fusion.30
  331.7 1.9 constant_dynamic-update-slice_fusion.29
  333.6 1.9 constant_dynamic-update-slice_fusion.28
  350.1 1.8 constant_dynamic-update-slice_fusion.14
  362.1 1.8 constant_dynamic-update-slice_fusion.2
  366.5 3.9 fusion.29
  370.5 43.1 %all-to-all-done.5 = bf16[16,32,2,2048]{3,2,0,1:T(2,128)(2,1)} async-done(((bf16[16,32,2,2048]{3,2,0,1:T(2,128)(2,1)}), bf16[16,32,2,2048]{3,2,0,1:T(2,128)(2,1)}, u32[]{:S(2)}, u32[]{:S(2)}) %all-to-all-start.5) | async-done | bytes 4194336 | tf_op jit(solution)/shard_map/all_to_all | solution.py:84
  413.6 8.0 %copy.70 = bf16[16,32,2,2048]{3,2,1,0:T(2,128)(2,1)} copy(bf16[16,32,2,2048]{3,2,0,1:T(2,128)(2,1)} %all-to-all-done.5) | data formatting | bytes 8388608 | tf_op jit(solution)/shard_map/all_to_all | solution.py:84
  421.6 7.2 %reshape.113 = bf16[1024,2048]{1,0:T(8,128)(2,1)} reshape(bf16[16,32,2,2048]{3,2,1,0:T(2,128)(2,1)} %copy.70) | data formatting | bytes 8388608 | tf_op jit(solution)/shard_map/reshape | solution.py:91
  428.7 7.2 %gather_fusion = bf16[512,2048]{1,0:T(8,128)(2,1)S(1)} fusion(bf16[1024,2048]{1,0:T(8,128)(2,1)} %reshape.113, s32[1024]{0:T(1024)S(1)} %pad_clamp_fusion), kind=kCustom, calls=%fused_computation | custom fusion | bytes 4196352 | tf_op jit(solution)/shard_map/gather | solution.py:92
  435.9 3.0 reshape.115
  439.0 4.8 %reduce_sum.19 = f32[128,2048]{1,0:T(8,128)S(1)} reduce(f32[128,4,2048]{2,1,0:T(4,128)} %reshape.115, f32[]{:T(128)} %constant.46.clone.1), dimensions={1}, to_apply=%region_5.6 | reduce | flops 786432 | bytes 5242884 | tf_op jit(solution)/shard_map/reduce_sum | solution.py:93
  443.8 5.9 %fusion.8 = bf16[128,1536]{1,0:T(8,128)(2,1)} fusion(f32[128,1536]{1,0:T(8,128)S(1)} %fusion.29, bf16[4096,1536]{0,1:T(8,128)(2,1)} %constant_dynamic-update-slice_fusion, s32[]{:T(128)S(6)} %select_n.32, f32[128,2048]{1,0:T(8,128)S(1)} %reduce_sum.19, f32[2048]{0:T(1024)S(1)} %copy-done.7, f32[128]{0:T(128)S(1)} %convert_divide_fusion, f32[1536]{0:T(1024)S(1)} %copy-done.8), kind=kOutput, calls=%fused_computation.9 | convolution fusion | flops 808255488 | bytes 8534532 | tf_op jit(solution)/shard_map/dot_general | solution.py:97
  (95 shorter events, 44.2 us)
Async XLA Ops:
  6.5 360.0 %copy-start = (bf16[128,1536]{1,0:T(8,128)(2,1)S(1)}, bf16[128,1536]{1,0:T(8,128)(2,1)}, u32[]{:S(2)}) copy-start(bf16[128,1536]{1,0:T(8,128)(2,1)} %param.19) | copy-start | bytes 1179652
  15.4 17.2 %all-to-all-start = ((bf16[16,32,2]{1,2,0:T(2,128)(2,1)}), bf16[16,32,2]{1,2,0:T(2,128)(2,1)S(1)}, u32[]{:S(2)}, u32[]{:S(2)}) async-start(bf16[16,32,2]{1,2,0:T(2,128)(2,1)} %copy.63), calls=%async_computation | async-start | bytes 16384 | tf_op jit(solution)/shard_map/all_to_all | solution.py:67
  32.7 15.8 %all-to-all-start.2 = ((bf16[16,32,2,128]{3,2,1,0:T(2,128)(2,1)}), bf16[16,32,2,128]{3,2,1,0:T(2,128)(2,1)S(1)}, u32[]{:S(2)}, u32[]{:S(2)}) async-start(bf16[16,32,2,128]{3,2,1,0:T(2,128)(2,1)} %bitcast.6), calls=%async_computation.2 | async-start | bytes 524288 | tf_op jit(solution)/shard_map/all_to_all | solution.py:60
  48.5 19.9 %all-to-all-start.1 = ((bf16[16,32,2]{0,2,1:T(2,128)(2,1)}), bf16[16,32,2]{0,2,1:T(2,128)(2,1)S(1)}, u32[]{:S(2)}, u32[]{:S(2)}) async-start(bf16[16,32,2]{0,2,1:T(2,128)(2,1)} %copy.64), calls=%async_computation.1 | async-start | bytes 32768 | tf_op jit(solution)/shard_map/all_to_all | solution.py:66
  68.4 13.6 %all-to-all-start.3 = ((bf16[16,32,2,128]{3,2,0,1:T(2,128)(2,1)}), bf16[16,32,2,128]{3,2,0,1:T(2,128)(2,1)S(1)}, u32[]{:S(2)}, u32[]{:S(2)}) async-start(bf16[16,32,2,128]{3,2,0,1:T(2,128)(2,1)} %copy.67), calls=%async_computation.3 | async-start | bytes 524288 | tf_op jit(solution)/shard_map/all_to_all | solution.py:59
  94.0 15.6 %copy-start.5 = (bf16[128,48]{0,1:T(8,128)(2,1)S(1)}, bf16[128,48]{0,1:T(8,128)(2,1)}, u32[]{:S(2)}) copy-start(bf16[128,48]{0,1:T(8,128)(2,1)} %param.16) | copy-start | bytes 36868
  94.0 134.7 %copy-start.6 = (bf16[96,48]{0,1:T(8,128)(2,1)S(1)}, bf16[96,48]{0,1:T(8,128)(2,1)}, u32[]{:S(2)}) copy-start(bf16[96,48]{0,1:T(8,128)(2,1)} %param.18) | copy-start | bytes 27652
  101.7 207.6 %all-to-all-start.4 = ((bf16[16,32,2,2048]{3,2,1,0:T(2,128)(2,1)}), bf16[16,32,2,2048]{3,2,1,0:T(2,128)(2,1)}, u32[]{:S(2)}, u32[]{:S(2)}) async-start(bf16[16,32,2,2048]{3,2,1,0:T(2,128)(2,1)} %reshape.112), calls=%async_computation.4 | async-start | bytes 8388608 | tf_op jit(solution)/shard_map/all_to_all | solution.py:85
  109.6 257.0 %all-gather.2.cloned.1.call-start = ((), (), s32[]{:S(2)}) async-start(), calls=%async_computation.6 | async-start | bytes 5013504 | tf_op jit(solution)/shard_map/all_gather | solution.py:103
  150.3 54.3 %collective-permute-start = (bf16[128,1536]{0,1:T(8,128)(2,1)S(1)}, bf16[128,1536]{0,1:T(8,128)(2,1)S(1)}, u32[]{:S(2)}, u32[]{:S(2)}) collective-permute-start(bf16[128,1536]{0,1:T(8,128)(2,1)S(1)} %all_gather.9), channel_id=1, source_target_pairs={{0,32},{32,64},{64,96},{96,128},{128,160},{160,192},{192,224},{224... | collective-permute-start | bytes 1179656 | tf_op jit(solution)/shard_map/ppermute | solution.py:13
  204.6 7.2 %collective-permute-start.1 = (bf16[128,1536]{0,1:T(8,128)(2,1)S(1)}, bf16[128,1536]{0,1:T(8,128)(2,1)S(1)}, u32[]{:S(2)}, u32[]{:S(2)}) collective-permute-start(bf16[128,1536]{0,1:T(8,128)(2,1)S(1)} %collective-permute-done), channel_id=1, source_target_pairs={{0,32},{32,64},{64,96},{96,128},{128,160},{160,192},{192,224},{224... | collective-permute-start | bytes 1179656 | tf_op jit(solution)/shard_map/ppermute | solution.py:13
  207.1 7.5 %collective-permute-start.8 = (bf16[128,1536]{0,1:T(8,128)(2,1)S(1)}, bf16[128,1536]{0,1:T(8,128)(2,1)S(1)}, u32[]{:S(2)}, u32[]{:S(2)}) collective-permute-start(bf16[128,1536]{0,1:T(8,128)(2,1)S(1)} %all_gather.9), channel_id=1, source_target_pairs={{0,480},{32,0},{64,32},{96,64},{128,96},{160,128},{192,160},{224,1... | collective-permute-start | bytes 1179656 | tf_op jit(solution)/shard_map/ppermute | solution.py:15
  211.8 7.2 %collective-permute-start.2 = (bf16[128,1536]{0,1:T(8,128)(2,1)S(1)}, bf16[128,1536]{0,1:T(8,128)(2,1)S(1)}, u32[]{:S(2)}, u32[]{:S(2)}) collective-permute-start(bf16[128,1536]{0,1:T(8,128)(2,1)S(1)} %collective-permute-done.1), channel_id=1, source_target_pairs={{0,32},{32,64},{64,96},{96,128},{128,160},{160,192},{192,224},{224... | collective-permute-start | bytes 1179656 | tf_op jit(solution)/shard_map/ppermute | solution.py:13
  214.6 7.5 %collective-permute-start.9 = (bf16[128,1536]{0,1:T(8,128)(2,1)S(1)}, bf16[128,1536]{0,1:T(8,128)(2,1)S(1)}, u32[]{:S(2)}, u32[]{:S(2)}) collective-permute-start(bf16[128,1536]{0,1:T(8,128)(2,1)S(1)} %collective-permute-done.8), channel_id=1, source_target_pairs={{0,480},{32,0},{64,32},{96,64},{128,96},{160,128},{192,160},{224,1... | collective-permute-start | bytes 1179656 | tf_op jit(solution)/shard_map/ppermute | solution.py:15
  219.0 7.2 %collective-permute-start.3 = (bf16[128,1536]{0,1:T(8,128)(2,1)S(1)}, bf16[128,1536]{0,1:T(8,128)(2,1)S(1)}, u32[]{:S(2)}, u32[]{:S(2)}) collective-permute-start(bf16[128,1536]{0,1:T(8,128)(2,1)S(1)} %collective-permute-done.2), channel_id=1, source_target_pairs={{0,32},{32,64},{64,96},{96,128},{128,160},{160,192},{192,224},{224... | collective-permute-start | bytes 1179656 | tf_op jit(solution)/shard_map/ppermute | solution.py:13
  222.1 49.2 %collective-permute-start.10 = (bf16[128,1536]{0,1:T(8,128)(2,1)S(1)}, bf16[128,1536]{0,1:T(8,128)(2,1)S(1)}, u32[]{:S(2)}, u32[]{:S(2)}) collective-permute-start(bf16[128,1536]{0,1:T(8,128)(2,1)S(1)} %collective-permute-done.9), channel_id=1, source_target_pairs={{0,480},{32,0},{64,32},{96,64},{128,96},{160,128},{192,160},{224,1... | collective-permute-start | bytes 1179656 | tf_op jit(solution)/shard_map/ppermute | solution.py:15
  226.3 61.2 %collective-permute-start.4 = (bf16[128,1536]{0,1:T(8,128)(2,1)S(1)}, bf16[128,1536]{0,1:T(8,128)(2,1)}, u32[]{:S(2)}, u32[]{:S(2)}) collective-permute-start(bf16[128,1536]{0,1:T(8,128)(2,1)S(1)} %collective-permute-done.3), channel_id=1, source_target_pairs={{0,32},{32,64},{64,96},{96,128},{128,160},{160,192},{192,224},{224... | collective-permute-start | bytes 1179656 | tf_op jit(solution)/shard_map/ppermute | solution.py:13
  271.4 17.4 %collective-permute-start.11 = (bf16[128,1536]{0,1:T(8,128)(2,1)S(1)}, bf16[128,1536]{0,1:T(8,128)(2,1)S(1)}, u32[]{:S(2)}, u32[]{:S(2)}) collective-permute-start(bf16[128,1536]{0,1:T(8,128)(2,1)S(1)} %collective-permute-done.10), channel_id=1, source_target_pairs={{0,480},{32,0},{64,32},{96,64},{128,96},{160,128},{192,160},{224,1... | collective-permute-start | bytes 1179656 | tf_op jit(solution)/shard_map/ppermute | solution.py:15
  287.5 6.0 %collective-permute-start.5 = (bf16[128,1536]{0,1:T(8,128)(2,1)}, bf16[128,1536]{0,1:T(8,128)(2,1)S(1)}, u32[]{:S(2)}, u32[]{:S(2)}) collective-permute-start(bf16[128,1536]{0,1:T(8,128)(2,1)} %collective-permute-done.4), channel_id=1, source_target_pairs={{0,32},{32,64},{64,96},{96,128},{128,160},{160,192},{192,224},{224... | collective-permute-start | bytes 1179656 | tf_op jit(solution)/shard_map/ppermute | solution.py:13
  288.8 0.7 copy-start.1
  289.5 7.3 %collective-permute-start.12 = (bf16[128,1536]{0,1:T(8,128)(2,1)S(1)}, bf16[128,1536]{0,1:T(8,128)(2,1)}, u32[]{:S(2)}, u32[]{:S(2)}) collective-permute-start(bf16[128,1536]{0,1:T(8,128)(2,1)S(1)} %collective-permute-done.11), channel_id=1, source_target_pairs={{0,480},{32,0},{64,32},{96,64},{128,96},{160,128},{192,160},{224,1... | collective-permute-start | bytes 1179656 | tf_op jit(solution)/shard_map/ppermute | solution.py:15
  293.5 3.4 copy-start.3
  293.5 13.9 %collective-permute-start.6 = (bf16[128,1536]{0,1:T(8,128)(2,1)S(1)}, bf16[128,1536]{0,1:T(8,128)(2,1)}, u32[]{:S(2)}, u32[]{:S(2)}) collective-permute-start(bf16[128,1536]{0,1:T(8,128)(2,1)S(1)} %collective-permute-done.5), channel_id=1, source_target_pairs={{0,32},{32,64},{64,96},{96,128},{128,160},{160,192},{192,224},{224... | collective-permute-start | bytes 1179656 | tf_op jit(solution)/shard_map/ppermute | solution.py:13
  296.9 27.0 %collective-permute-start.13 = (bf16[128,1536]{0,1:T(8,128)(2,1)}, bf16[128,1536]{0,1:T(8,128)(2,1)}, u32[]{:S(2)}, u32[]{:S(2)}) collective-permute-start(bf16[128,1536]{0,1:T(8,128)(2,1)} %collective-permute-done.12), channel_id=1, source_target_pairs={{0,480},{32,0},{64,32},{96,64},{128,96},{160,128},{192,160},{224,1... | collective-permute-start | bytes 1179656 | tf_op jit(solution)/shard_map/ppermute | solution.py:15
  307.4 20.7 %collective-permute-start.7 = (bf16[128,1536]{0,1:T(8,128)(2,1)}, bf16[128,1536]{0,1:T(8,128)(2,1)}, u32[]{:S(2)}, u32[]{:S(2)}) collective-permute-start(bf16[128,1536]{0,1:T(8,128)(2,1)} %collective-permute-done.6), channel_id=1, source_target_pairs={{0,32},{32,64},{64,96},{96,128},{128,160},{160,192},{192,224},{224... | collective-permute-start | bytes 1179656 | tf_op jit(solution)/shard_map/ppermute | solution.py:13
  318.1 95.5 %all-to-all-start.5 = ((bf16[16,32,2,2048]{3,2,0,1:T(2,128)(2,1)}), bf16[16,32,2,2048]{3,2,0,1:T(2,128)(2,1)}, u32[]{:S(2)}, u32[]{:S(2)}) async-start(bf16[16,32,2,2048]{3,2,0,1:T(2,128)(2,1)} %copy.69), calls=%async_computation.5 | async-start | bytes 8388608 | tf_op jit(solution)/shard_map/all_to_all | solution.py:84
  323.8 28.1 %copy-start.4 = (bf16[128,1536]{0,1:T(8,128)(2,1)S(1)}, bf16[128,1536]{0,1:T(8,128)(2,1)}, u32[]{:S(2)}) copy-start(bf16[128,1536]{0,1:T(8,128)(2,1)} %copy-done.3) | copy-start | bytes 1179652
  323.8 37.4 %copy-start.2 = (bf16[128,1536]{0,1:T(8,128)(2,1)S(1)}, bf16[128,1536]{0,1:T(8,128)(2,1)}, u32[]{:S(2)}) copy-start(bf16[128,1536]{0,1:T(8,128)(2,1)} %copy-done.1) | copy-start | bytes 1179652
  323.9 23.6 %collective-permute-start.14 = (bf16[128,1536]{0,1:T(8,128)(2,1)}, bf16[128,1536]{0,1:T(8,128)(2,1)S(1)}, u32[]{:S(2)}, u32[]{:S(2)}) collective-permute-start(bf16[128,1536]{0,1:T(8,128)(2,1)} %collective-permute-done.13), channel_id=1, source_target_pairs={{0,480},{32,0},{64,32},{96,64},{128,96},{160,128},{192,160},{224,1... | collective-permute-start | bytes 1179656 | tf_op jit(solution)/shard_map/ppermute | solution.py:15
  428.7 15.1 %copy-start.7 = (f32[2048]{0:T(1024)S(1)}, f32[2048]{0:T(1024)}, u32[]{:S(2)}) copy-start(f32[2048]{0:T(1024)} %param.15) | copy-start | bytes 24580
  428.7 15.1 %copy-start.8 = (f32[1536]{0:T(1024)S(1)}, f32[1536]{0:T(1024)}, u32[]{:S(2)}) copy-start(f32[1536]{0:T(1024)} %param.17) | copy-start | bytes 18436
Sparse Core Ops, SparseCore 0:
  271.5 61.1 all-gather.1
